TPU v7x, 256 devices: a whole 4x4x8 slice. The times are simulated.
256 devices in a mesh: inst: 4 (over x_lo, core), space: 64 (over x_hi, z, y).
Axes of the slice: x: 4 (x_hi: 2, x_lo: 2; x = x_hi * 2 + x_lo), y: 4, z: 8, core: 2. Of those that a mesh axis runs over, the one named last changes fastest.
Arguments:
- flow_state: float32 [8, 5, 4096, 256], P('inst', None, 'space'), may hold values from -6 to 6
- flow_source: float32 [8, 5, 4096, 256], P('inst', None, 'space'), may hold values from -6 to 6
- pseudo_step: float32 [4096, 256], P('space'), may hold values from 0.03 to 0.12
- flux_jacobian: float32 [5, 5], replicated, may hold values from -2.5 to 2.5
- stator_donor: int32 [8, 4096], P('inst', 'space'), may hold values from 0 to 4095, as said below
- stator_weight: float32 [8, 4096], P('inst', 'space'), may hold values from 0 to 1
- rotor_donor: int32 [8, 4096], P('inst', 'space'), may hold values from 0 to 4095, as said below
- rotor_weight: float32 [8, 4096], P('inst', 'space'), may hold values from 0 to 1
Outputs:
- new_state: float32 [8, 5, 4096, 256], P('inst', None, 'space')
- residual: float32 [8, 5, 4096, 256], P('inst', None, 'space')
Inputs may be any that keep to these rules, and one draw needn't show every extreme that they name: `stator_donor`: for each instance n the row holds the rotation j -> (j - shift_n) mod 4096 of the rows, so entry j is (j - stator_shift_n) mod 4096, where stator_shift_n is a shift of its own for each instance. `rotor_donor`: for each instance n the row holds the rotation j -> (j + shift_n) mod 4096 of the rows, so entry j is (j + rotor_shift_n) mod 4096, where rotor_shift_n is a shift of its own for each instance, independent of stator_shift_n.
All inputs are finite; a program needn't handle non-finite values.
Results may differ from a plain program's by a relative error of at most 0.0001.
Values sent between devices are 32-bit elements; how exact they have to be, the bound alone decides.
A program may use at most 128 MiB of HBM per device.

v0:
```python
import math
import jax
import jax.numpy as jnp
from jax import lax
from jax.sharding import PartitionSpec as P

NT = 8
SWEEPS = 2
viscosity = 0.5


def with_halo(x, sides, width):
    for axis, dim in sides:
        count, length = (lax.axis_size(axis), x.shape[dim])
        up = [(i, (i + 1) % count) for i in range(count)]
        down = [(j, i) for i, j in up]
        last = lax.slice_in_dim(x, length - width, length, axis=dim)
        leading = lax.slice_in_dim(x, 0, width, axis=dim)
        before = lax.ppermute(last, axis, up)
        after = lax.ppermute(leading, axis, down)
        x = jnp.concatenate([before, x, after], axis=dim)
    return x


def spectral_table(count):
    rows = jnp.arange(count, dtype=jnp.int32)[:, None]
    columns = jnp.arange(count, dtype=jnp.int32)[None, :]
    gap = rows - columns
    parity = (1 - 2 * (gap % 2)).astype(jnp.float32)
    angle = math.pi / count * gap.astype(jnp.float32)
    sine = jnp.where(gap == 0, jnp.float32(1.0), jnp.sin(angle))
    value = 0.5 * parity * jnp.cos(angle) / sine
    return jnp.where(gap == 0, jnp.float32(0.0), value)


def interpolate(column, donor, weight):
    total = column.shape[2]
    first = jnp.take_along_axis(column, donor[:, None, :], axis=2)
    second = jnp.take_along_axis(column, ((donor + 1) % total)[:, None, :], axis=2)
    return (1.0 - weight)[:, None, :] * first + weight[:, None, :] * second


def spatial(flow, upper, lower, stator_in, rotor_in, flux_jacobian):
    half = flow.shape[3] // 2
    zero_col = jnp.zeros(flow.shape[:3] + (1,), jnp.float32)
    left_cells = jnp.concatenate([zero_col, flow[..., :-1]], axis=3).at[..., half].set(stator_in)
    right_cells = jnp.concatenate([flow[..., 1:], zero_col], axis=3).at[..., half - 1].set(rotor_in)
    convect = jnp.einsum(
        "vw,nwca->nvca", flux_jacobian, flow - left_cells, precision=lax.Precision.HIGHEST
    )
    return convect + viscosity * (4.0 * flow - left_cells - right_cells - upper - lower)


def apply_columns(local_rows, piece):
    return jnp.einsum("nm,mvca->nvca", local_rows, piece, precision=lax.Precision.HIGHEST)


def local(
    flow_state,
    flow_source,
    pseudo_step,
    flux_jacobian,
    stator_donor,
    stator_weight,
    rotor_donor,
    rotor_weight,
):
    local_count = flow_state.shape[0]
    position = lax.axis_index("inst")
    table = spectral_table(NT)
    half = flow_state.shape[3] // 2
    local_rows = lax.dynamic_slice_in_dim(table, position * local_count, local_count, 0)
    flow = flow_state
    residual = flow
    for sweep in range(SWEEPS):
        rotor_all, stator_all = (
            lax.all_gather(flow[..., half - 1], "space", axis=2, tiled=True),
            lax.all_gather(flow[..., half], "space", axis=2, tiled=True),
        )
        stator_in = interpolate(rotor_all, stator_donor, stator_weight)
        rotor_in = interpolate(stator_all, rotor_donor, rotor_weight)
        padded = with_halo(flow, (("space", 2),), 1)
        upper = padded[:, :, :-2]
        lower = padded[:, :, 2:]
        derivative = apply_columns(local_rows, lax.all_gather(flow, "inst", axis=0, tiled=True))
        residual = (
            spatial(flow, upper, lower, stator_in, rotor_in, flux_jacobian)
            + derivative
            - flow_source
        )
        flow = flow - pseudo_step[None, None] * residual
    return (flow, residual)


def solution(mesh):
    return jax.shard_map(
        local,
        mesh=mesh,
        in_specs=(
            P("inst", None, "space", None),
            P("inst", None, "space", None),
            P("space", None),
            P(),
            P("inst", "space"),
            P("inst", "space"),
            P("inst", "space"),
            P("inst", "space"),
        ),
        out_specs=(P("inst", None, "space", None), P("inst", None, "space", None)),
        check_vma=False,
    )
```

profile of v0, /device:TPU:6, one launch (start us, length us, event | category | flops | bytes accessed | tf_op | source)
XLA Modules:
  0.0 1462.7 jit_solution(14926466707886030366)
XLA Ops:
  11.2 7.7 collective-permute-start.1
  21.7 212.1 %all-gather = f32[2,5,4096,1]{1,2,0,3:T(8,128)} all-gather(f32[2,5,64,1]{1,2,0,3:T(8,128)S(1)} %copy.137), channel_id=2, replica_groups=mesh['inst'=4,'space'=64] {'space'}, dimensions={2}, use_global_device_ids=true | all-gather | bytes 166400 | tf_op jit(solution)/shard_map/all_gather | solution.py:77
  235.7 1.8 gather_fusion
  238.9 209.7 %all-gather.1 = f32[2,5,4096,1]{1,2,0,3:T(8,128)} all-gather(f32[2,5,64,1]{1,2,0,3:T(8,128)S(1)} %copy.138), channel_id=3, replica_groups=mesh['inst'=4,'space'=64] {'space'}, dimensions={2}, use_global_device_ids=true | all-gather | bytes 166400 | tf_op jit(solution)/shard_map/all_gather | solution.py:78
  448.6 1.8 gather_fusion.2
  450.5 1.8 gather_fusion.3
  455.2 1.8 scatter.14
  457.0 12.3 scatter.15
  469.4 5.3 fusion.2
  474.8 3.9 fusion.5
  479.9 453.1 %all-gather.2 = f32[2,5,4096,1]{3,1,2,0:T(8,128)} all-gather(f32[2,5,64,1]{3,1,2,0:T(8,128)S(1)} %get-tuple-element.59), channel_id=4, replica_groups=mesh['inst'=4,'space'=64] {'space'}, dimensions={2}, use_global_device_ids=true | all-gather | bytes 166400 | tf_op jit(solution)/shard_map/all_gather | solution.py:77
  933.0 17.8 %copy.117 = f32[2,5,4096,1]{2,0,1,3:T(2,128)S(1)} copy(f32[2,5,4096,1]{3,1,2,0:T(8,128)} %all-gather.2) | data formatting | bytes 327680 | tf_op jit(solution)/shard_map/all_gather | solution.py:77
  950.8 2.7 copy.118
  957.0 436.0 %all-gather.3 = f32[2,5,4096,1]{3,1,2,0:T(8,128)} all-gather(f32[2,5,64,1]{3,1,2,0:T(8,128)S(1)} %get-tuple-element.60), channel_id=5, replica_groups=mesh['inst'=4,'space'=64] {'space'}, dimensions={2}, use_global_device_ids=true | all-gather | bytes 166400 | tf_op jit(solution)/shard_map/all_gather | solution.py:78
  1393.1 17.8 %copy.123 = f32[2,5,4096,1]{2,0,1,3:T(2,128)S(1)} copy(f32[2,5,4096,1]{3,1,2,0:T(8,128)} %all-gather.3) | data formatting | bytes 327680 | tf_op jit(solution)/shard_map/all_gather | solution.py:78
  1410.8 2.7 copy.124
  1413.5 1.8 gather_fusion.6
  1415.3 1.8 gather_fusion.7
  1420.4 2.3 concatenate.39
  1422.7 7.7 collective-permute-start.3
  1430.4 1.8 scatter.16
  1432.2 12.3 scatter.19
  1444.6 5.3 fusion
  1449.9 3.9 multiply_subtract_fusion
  (75 shorter events, 23.4 us)
Async XLA Ops:
  7.2 467.6 %copy-start = (f32[5,5]{1,0:T(8,128)S(1)}, f32[5,5]{1,0:T(8,128)}, u32[]{:S(2)}) copy-start(f32[5,5]{1,0:T(8,128)} %param.21) | copy-start | bytes 304
  7.2 462.2 %all-gather.7.cloned.1.call-start = ((), (), s32[]{:S(2)}) async-start(), calls=%async_computation | async-start | bytes 3276800 | tf_op jit(solution)/shard_map/all_gather | solution.py:85
  7.9 229.6 %copy-start.7 = (s32[2,64]{1,0:T(2,128)S(1)}, s32[2,64]{1,0:T(2,128)}, u32[]{:S(2)}) copy-start(s32[2,64]{1,0:T(2,128)} %param.22) | copy-start | bytes 1540
  7.9 229.7 %copy-start.5 = (f32[2,64]{1,0:T(2,128)S(1)}, f32[2,64]{1,0:T(2,128)}, u32[]{:S(2)}) copy-start(f32[2,64]{1,0:T(2,128)} %param.23) | copy-start | bytes 1540
  7.9 230.8 %copy-start.8 = (s32[2,64]{1,0:T(2,128)S(1)}, s32[2,64]{1,0:T(2,128)}, u32[]{:S(2)}) copy-start(s32[2,64]{1,0:T(2,128)} %param.24) | copy-start | bytes 1540
  7.9 1436.6 %all-gather.9.cloned.1.call-start = ((), (), s32[]{:S(2)}) async-start(), calls=%async_computation.1 | async-start | bytes 3276800 | tf_op jit(solution)/shard_map/all_gather | solution.py:85
  9.5 465.2 %collective-permute-start = (f32[2,5,1,256]{3,1,2,0:T(8,128)S(1)}, f32[2,5,1,256]{3,1,2,0:T(8,128)S(1)}, u32[]{:S(2)}, u32[]{:S(2)}) collective-permute-start(f32[2,5,1,256]{3,1,2,0:T(8,128)S(1)} %get-tuple-element.67), channel_id=1, source_target_pairs={{0,1},{1,2},{2,3},{3,4},{4,5},{5,6},{6,7},{7,8},{8,9},{9,10},{10,1... | collective-permute-start | bytes 30728 | tf_op jit(solution)/shard_map/ppermute | solution.py:19
  11.2 463.6 %collective-permute-start.1 = (f32[2,5,1,256]{3,1,2,0:T(8,128)S(1)}, f32[2,5,1,256]{3,1,2,0:T(8,128)S(1)}, u32[]{:S(2)}, u32[]{:S(2)}) collective-permute-start(f32[2,5,1,256]{3,1,2,0:T(8,128)S(1)} %get-tuple-element.68), channel_id=1, source_target_pairs={{1,0},{2,1},{3,2},{4,3},{5,4},{6,5},{7,6},{8,7},{9,8},{10,9},{11,1... | collective-permute-start | bytes 30728 | tf_op jit(solution)/shard_map/ppermute | solution.py:20
  21.7 430.7 %copy-start.6 = (f32[2,64]{1,0:T(2,128)S(1)}, f32[2,64]{1,0:T(2,128)}, u32[]{:S(2)}) copy-start(f32[2,64]{1,0:T(2,128)} %param.25) | copy-start | bytes 1540
  454.2 20.6 %copy-start.1 = (f32[2,5,64,256]{3,2,1,0:T(8,128)S(1)}, f32[2,5,64,256]{3,2,1,0:T(8,128)}, u32[]{:S(2)}) copy-start(f32[2,5,64,256]{3,2,1,0:T(8,128)} %param.19) | copy-start | bytes 1966084
  454.2 20.6 %copy-start.4 = (f32[64,256]{1,0:T(8,128)S(1)}, f32[64,256]{1,0:T(8,128)}, u32[]{:S(2)}) copy-start(f32[64,256]{1,0:T(8,128)} %param.20) | copy-start | bytes 196612
  457.0 17.7 %copy-start.3 = (f32[2,5,64,256]{3,1,2,0:T(8,128)}, f32[2,5,64,256]{3,1,2,0:T(8,128)S(1)}, u32[]{:S(2)}) copy-start(f32[2,5,64,256]{3,1,2,0:T(8,128)S(1)} %scatter.14) | copy-start | bytes 1966084
  1422.7 27.2 %collective-permute-start.2 = (f32[2,5,1,256]{3,1,2,0:T(8,128)S(1)}, f32[2,5,1,256]{3,1,2,0:T(8,128)S(1)}, u32[]{:S(2)}, u32[]{:S(2)}) collective-permute-start(f32[2,5,1,256]{3,1,2,0:T(8,128)S(1)} %get-tuple-element.63), channel_id=1, source_target_pairs={{0,1},{1,2},{2,3},{3,4},{4,5},{5,6},{6,7},{7,8},{8,9},{9,10},{10,1... | collective-permute-start | bytes 30728 | tf_op jit(solution)/shard_map/ppermute | solution.py:19
  1422.7 27.2 %collective-permute-start.3 = (f32[2,5,1,256]{3,1,2,0:T(8,128)S(1)}, f32[2,5,1,256]{3,1,2,0:T(8,128)S(1)}, u32[]{:S(2)}, u32[]{:S(2)}) collective-permute-start(f32[2,5,1,256]{3,1,2,0:T(8,128)S(1)} %get-tuple-element.64), channel_id=1, source_target_pairs={{1,0},{2,1},{3,2},{4,3},{5,4},{6,5},{7,6},{8,7},{9,8},{10,9},{11,1... | collective-permute-start | bytes 30728 | tf_op jit(solution)/shard_map/ppermute | solution.py:20
  1432.2 12.3 copy-start.2
Sparse Core Ops, SparseCore 0:
  9.8 38.0 all-gather.6
  479.9 29.6 all-gather.8
where the time goes:
time: 1460 us
  blocking collectives  1310 us (90%)
  local copies, waits for them, and re-layouts  100 us (7%)
  matrix products  18.4 us (1%)
  starting transfers between devices  17.1 us (1%)
    all_gather x2, blocking collectives, local(): lax.all_gather(flow[..., half - 1], 'space', axis=2, tiled=True)  665 us
    all_gather x2, blocking collectives, local(): lax.all_gather(flow[..., half], 'space', axis=2, tiled=True)  646 us
  transfers between devices with their start and end apart: 6, of which 0 were waited for; matrix products, arithmetic and copies ran while one was open for 7% of the time, Pallas kernels for 0%

commit v1 on v0

--- a/solution.py
+++ b/solution.py
@@ -3,6 +3,7 @@
 import jax.numpy as jnp
 from jax import lax
 from jax.sharding import PartitionSpec as P
+from jax.lax import all_to_all, axis_size
 
 NT = 8
 SWEEPS = 2
@@ -73,9 +74,18 @@
     flow = flow_state
     residual = flow
     for sweep in range(SWEEPS):
+        track_the_sheets = lambda local_x, ndim_at: jnp.concatenate(
+            all_to_all(
+                jnp.stack([local_x for _ in range(axis_size("space"))], axis=0),
+                axis_name="space",
+                split_axis=0,
+                concat_axis=0,
+            ),
+            axis=ndim_at,
+        )
         rotor_all, stator_all = (
             lax.all_gather(flow[..., half - 1], "space", axis=2, tiled=True),
-            lax.all_gather(flow[..., half], "space", axis=2, tiled=True),
+            track_the_sheets(flow[..., half], ndim_at=2),
         )
         stator_in = interpolate(rotor_all, stator_donor, stator_weight)
         rotor_in = interpolate(stator_all, rotor_donor, rotor_weight)

time: 1460 us -> 827 us (0.57)
  blocking collectives: 1310 us -> 667 us
  starting transfers between devices: 17.1 us -> 35.8 us
    all_gather x2 -> x0, blocking collectives: 646 us -> none  [local(): lax.all_gather(flow[..., half], 'space', axis=2, tiled=True)]
    all_gather x2 -> x0, local copies, waits for them, and re-layouts: 20.5 us -> none  [local(): lax.all_gather(flow[..., half], 'space', axis=2, tiled=True)]
    all_to_all x0 -> x2, starting transfers between devices: none -> 20.2 us  [local(): all_to_all(jnp.stack([local_x for _ in range(axis_size('space'))], axis=0...]
  transfers between devices with their start and end apart: 6 -> 8, of which waited for: 0 -> 0; matrix products, arithmetic and copies ran while one was open for 7% -> 12% of each run, Pallas kernels for 0% -> 0%
where the time goes in v1:
time: 827 us
  blocking collectives  667 us (81%)
  local copies, waits for them, and re-layouts  87.1 us (11%)
  starting transfers between devices  35.8 us (4%)
  matrix products  18.9 us (2%)
  between operations  14.5 us (2%)
    all_gather x2, blocking collectives, local(): lax.all_gather(flow[..., half - 1], 'space', axis=2, tiled=True)  667 us
    scatter x2, local copies, waits for them, and re-layouts, spatial(): jnp.concatenate([flow[..., 1:], zero_col], axis=3).at[..., half - 1]  20.8 us
    all_gather x2, local copies, waits for them, and re-layouts, local(): lax.all_gather(flow[..., half - 1], 'space', axis=2, tiled=True)  20.5 us
    all_to_all x2, starting transfers between devices, local(): all_to_all(jnp.stack([local_x for _ in range(axis_size('space'))], axis=0...  20.2 us
  transfers between devices with their start and end apart: 8, of which 0 were waited for; matrix products, arithmetic and copies ran while one was open for 12% of the time, Pallas kernels for 0%

profile of v1, /device:TPU:6, one launch (start us, length us, event | category | flops | bytes accessed | tf_op | source)
XLA Modules:
  0.0 826.7 jit_solution(7323085985488087305)
XLA Ops:
  10.4 14.7 %all-to-all-start = ((f32[64,1,640]{2,1,0:T(1,128)}), f32[64,1,640]{2,1,0:T(1,128)S(1)}, u32[]{:S(2)}, u32[]{:S(2)}) async-start(f32[64,1,640]{2,1,0:T(1,128)} %reshape.329), calls=%async_computation | async-start | bytes 327680 | tf_op jit(solution)/shard_map/all_to_all | solution.py:78
  28.3 6.3 collective-permute-start.1
  35.7 208.8 %all-gather = f32[2,5,4096,1]{1,2,0,3:T(8,128)} all-gather(f32[2,5,64,1]{1,2,0,3:T(8,128)S(1)} %copy.137), channel_id=2, replica_groups=mesh['inst'=4,'space'=64] {'space'}, dimensions={2}, use_global_device_ids=true | all-gather | bytes 166400 | tf_op jit(solution)/shard_map/all_gather | solution.py:87
  244.5 1.8 gather_fusion.1
  246.4 1.8 gather_fusion
  250.4 3.0 scatter.14
  255.6 2.8 copy.106
  258.3 1.8 gather_fusion.2
  260.2 1.8 gather_fusion.3
  262.3 10.4 %scatter.15 = f32[2,5,64,256]{3,1,2,0:T(8,128)S(1)} dynamic-update-slice(f32[2,5,64,256]{3,1,2,0:T(8,128)S(1)} %concatenate.35, f32[2,5,64,1]{3,1,2,0:T(8,128)S(1)} %copy.109, s32[]{:T(128)} %constant.160.clone.1, s32[]{:T(128)} %constant.160.clone.1, s32[]{:T(128)} %constant.160.clone.1, s32[]{:T(128)} %constant.165.clone.1) | dynamic-update-slice | bytes 5124 | tf_op jit(solution)/shard_map/scatter | solution.py:48
  272.8 5.6 fusion.2
  278.5 4.0 fusion.5
  283.7 457.8 %all-gather.1 = f32[2,5,4096,1]{3,1,2,0:T(8,128)} all-gather(f32[2,5,64,1]{3,1,2,0:T(8,128)S(1)} %get-tuple-element.59), channel_id=3, replica_groups=mesh['inst'=4,'space'=64] {'space'}, dimensions={2}, use_global_device_ids=true | all-gather | bytes 166400 | tf_op jit(solution)/shard_map/all_gather | solution.py:87
  741.5 17.8 %copy.118 = f32[2,5,4096,1]{2,0,1,3:T(2,128)S(1)} copy(f32[2,5,4096,1]{3,1,2,0:T(8,128)} %all-gather.1) | data formatting | bytes 327680 | tf_op jit(solution)/shard_map/all_gather | solution.py:87
  759.3 2.7 copy.119
  762.0 1.8 gather_fusion.4
  763.8 1.8 gather_fusion.5
  767.1 5.5 all-to-all-start.1
  778.9 6.3 collective-permute-start.3
  785.2 3.0 scatter.16
  789.6 2.8 copy.125
  797.0 10.4 %scatter.19 = f32[2,5,64,256]{3,1,2,0:T(8,128)S(1)} dynamic-update-slice(f32[2,5,64,256]{3,1,2,0:T(8,128)S(1)} %concatenate.39, f32[2,5,64,1]{3,1,2,0:T(8,128)S(1)} %copy.128, s32[]{:T(128)} %constant.160.clone.1, s32[]{:T(128)} %constant.160.clone.1, s32[]{:T(128)} %constant.160.clone.1, s32[]{:T(128)} %constant.165.clone.1) | dynamic-update-slice | bytes 5124 | tf_op jit(solution)/shard_map/scatter | solution.py:48
  808.4 5.3 fusion
  813.7 4.0 multiply_subtract_fusion
  (101 shorter events, 30.5 us)
Async XLA Ops:
  7.2 271.3 %copy-start = (f32[5,5]{1,0:T(8,128)S(1)}, f32[5,5]{1,0:T(8,128)}, u32[]{:S(2)}) copy-start(f32[5,5]{1,0:T(8,128)} %param.21) | copy-start | bytes 304
  7.2 27.4 %copy-start.14 = (s32[2,64]{1,0:T(2,128)S(1)}, s32[2,64]{1,0:T(2,128)}, u32[]{:S(2)}) copy-start(s32[2,64]{1,0:T(2,128)} %param.24) | copy-start | bytes 1540
  7.2 28.4 %copy-start.13 = (s32[2,64]{1,0:T(2,128)S(1)}, s32[2,64]{1,0:T(2,128)}, u32[]{:S(2)}) copy-start(s32[2,64]{1,0:T(2,128)} %param.22) | copy-start | bytes 1540
  7.2 265.6 %all-gather.5.cloned.1.call-start = ((), (), s32[]{:S(2)}) async-start(), calls=%async_computation.2 | async-start | bytes 3276800 | tf_op jit(solution)/shard_map/all_gather | solution.py:95
  9.2 239.2 %copy-start.5 = (f32[2,64]{1,0:T(2,128)S(1)}, f32[2,64]{1,0:T(2,128)}, u32[]{:S(2)}) copy-start(f32[2,64]{1,0:T(2,128)} %param.23) | copy-start | bytes 1540
  10.4 243.1 %all-to-all-start = ((f32[64,1,640]{2,1,0:T(1,128)}), f32[64,1,640]{2,1,0:T(1,128)S(1)}, u32[]{:S(2)}, u32[]{:S(2)}) async-start(f32[64,1,640]{2,1,0:T(1,128)} %reshape.329), calls=%async_computation | async-start | bytes 327680 | tf_op jit(solution)/shard_map/all_to_all | solution.py:78
  25.2 783.3 %all-gather.7.cloned.1.call-start = ((), (), s32[]{:S(2)}) async-start(), calls=%async_computation.3 | async-start | bytes 3276800 | tf_op jit(solution)/shard_map/all_gather | solution.py:95
  26.8 251.7 %collective-permute-start = (f32[2,5,1,256]{3,1,2,0:T(8,128)S(1)}, f32[2,5,1,256]{3,1,2,0:T(8,128)S(1)}, u32[]{:S(2)}, u32[]{:S(2)}) collective-permute-start(f32[2,5,1,256]{3,1,2,0:T(8,128)S(1)} %get-tuple-element.67), channel_id=1, source_target_pairs={{0,1},{1,2},{2,3},{3,4},{4,5},{5,6},{6,7},{7,8},{8,9},{9,10},{10,1... | collective-permute-start | bytes 30728 | tf_op jit(solution)/shard_map/ppermute | solution.py:20
  28.3 250.2 %collective-permute-start.1 = (f32[2,5,1,256]{3,1,2,0:T(8,128)S(1)}, f32[2,5,1,256]{3,1,2,0:T(8,128)S(1)}, u32[]{:S(2)}, u32[]{:S(2)}) collective-permute-start(f32[2,5,1,256]{3,1,2,0:T(8,128)S(1)} %get-tuple-element.68), channel_id=1, source_target_pairs={{1,0},{2,1},{3,2},{4,3},{5,4},{6,5},{7,6},{8,7},{9,8},{10,9},{11,1... | collective-permute-start | bytes 30728 | tf_op jit(solution)/shard_map/ppermute | solution.py:21
  248.3 2.1 copy-start.9
  248.4 2.1 copy-start.11
  248.7 4.9 copy-start.6
  253.5 25.0 %copy-start.7 = (pred[2,64]{1,0:T(4,128)(4,1)}, pred[2,64]{1,0:T(4,128)(4,1)S(1)}, u32[]{:S(2)}) copy-start(pred[2,64]{1,0:T(4,128)(4,1)S(1)} %get-tuple-element.75) | copy-start | bytes 388
  253.5 25.0 %copy-start.8 = (pred[2,64]{1,0:T(4,128)(4,1)}, pred[2,64]{1,0:T(4,128)(4,1)S(1)}, u32[]{:S(2)}) copy-start(pred[2,64]{1,0:T(4,128)(4,1)S(1)} %get-tuple-element.76) | copy-start | bytes 388
  255.5 23.0 %copy-start.1 = (f32[2,5,64,256]{3,2,1,0:T(8,128)S(1)}, f32[2,5,64,256]{3,2,1,0:T(8,128)}, u32[]{:S(2)}) copy-start(f32[2,5,64,256]{3,2,1,0:T(8,128)} %param.19) | copy-start | bytes 1966084
  255.6 23.0 %copy-start.4 = (f32[64,256]{1,0:T(8,128)S(1)}, f32[64,256]{1,0:T(8,128)}, u32[]{:S(2)}) copy-start(f32[64,256]{1,0:T(8,128)} %param.20) | copy-start | bytes 196612
  272.8 5.7 copy-start.3
  762.0 11.9 %copy-start.10 = (pred[2,64]{1,0:T(4,128)(4,1)S(1)}, pred[2,64]{1,0:T(4,128)(4,1)}, u32[]{:S(2)}) copy-start(pred[2,64]{1,0:T(4,128)(4,1)} %copy-done.9) | copy-start | bytes 388
  762.0 11.9 %copy-start.12 = (pred[2,64]{1,0:T(4,128)(4,1)S(1)}, pred[2,64]{1,0:T(4,128)(4,1)}, u32[]{:S(2)}) copy-start(pred[2,64]{1,0:T(4,128)(4,1)} %copy-done.11) | copy-start | bytes 388
  767.1 21.1 %all-to-all-start.1 = ((f32[64,1,640]{2,1,0:T(1,128)}), f32[64,1,640]{2,1,0:T(1,128)S(1)}, u32[]{:S(2)}, u32[]{:S(2)}) async-start(f32[64,1,640]{2,1,0:T(1,128)} %reshape.331), calls=%async_computation.1 | async-start | bytes 327680 | tf_op jit(solution)/shard_map/all_to_all | solution.py:78
  777.5 36.2 %collective-permute-start.2 = (f32[2,5,1,256]{3,1,2,0:T(8,128)}, f32[2,5,1,256]{3,1,2,0:T(8,128)S(1)}, u32[]{:S(2)}, u32[]{:S(2)}) collective-permute-start(f32[2,5,1,256]{3,1,2,0:T(8,128)} %get-tuple-element.63), channel_id=1, source_target_pairs={{0,1},{1,2},{2,3},{3,4},{4,5},{5,6},{6,7},{7,8},{8,9},{9,10},{10,1... | collective-permute-start | bytes 30728 | tf_op jit(solution)/shard_map/ppermute | solution.py:20
  778.9 34.8 %collective-permute-start.3 = (f32[2,5,1,256]{3,1,2,0:T(8,128)}, f32[2,5,1,256]{3,1,2,0:T(8,128)}, u32[]{:S(2)}, u32[]{:S(2)}) collective-permute-start(f32[2,5,1,256]{3,1,2,0:T(8,128)} %get-tuple-element.64), channel_id=1, source_target_pairs={{1,0},{2,1},{3,2},{4,3},{5,4},{6,5},{7,6},{8,7},{9,8},{10,9},{11,1... | collective-permute-start | bytes 30728 | tf_op jit(solution)/shard_map/ppermute | solution.py:21
  807.4 1.0 copy-start.2
Sparse Core Ops, SparseCore 0:
  9.8 39.8 all-gather.4
  283.7 30.3 all-gather.6
